TPU v7x, 512 devices: a whole 4x8x8 slice. The times are simulated.
512 devices in a mesh: src: 16 (over z, y_hi), tgt: 32 (over x, y_lo, core).
Axes of the slice: x: 4, y: 8 (y_hi: 2, y_lo: 4; y = y_hi * 4 + y_lo), z: 8, core: 2. Of those that a mesh axis runs over, the one named last changes fastest.
Arguments:
- hidden_in: bfloat16 [8192, 4096], P('tgt', 'src'), may hold values from -6 to 6
- norm_gain: bfloat16 [4096], replicated, may hold values from 0.25 to 1.75
- w_query: bfloat16 [4096, 4096], P(None, 'src'), may hold values from -0.09375 to 0.09375
- keys_cache: bfloat16 [4096, 4096], P('tgt', 'src')
- values_cache: bfloat16 [4096, 4096], P('tgt', 'src'), may hold values from -6 to 6
- lengths: int32 [16], replicated, may hold values from 1 to 256, 2560 in all
- w_output: bfloat16 [4096, 4096], P(None, 'src'), may hold values from -1.5 to 1.5
Outputs:
- hidden_out: float32 [8192, 4096], P('tgt', 'src')
Inputs may be any that keep to these rules, and one draw needn't show every extreme that they name: `lengths`: the source holds 16 responses of 256 positions each, response r at positions r * 256 onward; one response is full in every draw.
All inputs are finite; a program needn't handle non-finite values.
Results may differ from a plain program's by a relative error of at most 0.035.
Values may be sent and summed in bfloat16 or wider, within the bound.
A program may use at most 128 MiB of HBM per device.

v0:
```python
import jax
import jax.numpy as jnp
from jax import lax
from jax.sharding import PartitionSpec as P

HD = 64


def allowed_rows(offset, count, lengths, slot_size):
    positions = offset + jnp.arange(count, dtype=jnp.int32)
    owners = positions // slot_size
    within = positions % slot_size
    table = jnp.where(
        owners[:, None] == jnp.arange(lengths.shape[0], dtype=jnp.int32)[None, :],
        lengths[None, :],
        0,
    )
    return within < jnp.sum(table, axis=1)


def absorb(running, queries3, key_part, value_part, allowed):
    best, total, accum = running
    scores = jnp.einsum(
        "rhd,khd->hrk", queries3, key_part, preferred_element_type=jnp.float32
    ) * HD ** (-0.5)
    scores = jnp.where(allowed[None, None, :], scores, -1e30)
    fresh = jnp.maximum(best, jnp.max(scores, axis=2))
    factor = jnp.exp(best - fresh)
    expd = jnp.where(allowed[None, None, :], jnp.exp(scores - fresh[:, :, None]), 0.0)
    total = total * factor + jnp.sum(expd, axis=2)
    weighted = jnp.einsum(
        "hrk,khd->rhd", expd.astype(jnp.bfloat16), value_part, preferred_element_type=jnp.float32
    )
    accum = accum * factor.T[:, :, None] + weighted
    return (fresh, total, accum)


def start_state(heads_here, rows_count):
    return (
        jnp.full((heads_here, rows_count), -1e30, jnp.float32),
        jnp.zeros((heads_here, rows_count), jnp.float32),
        jnp.zeros((rows_count, heads_here, HD), jnp.float32),
    )


def body(hidden_in, norm_gain, w_query, keys_cache, values_cache, lengths, w_output):
    gathered = lax.all_gather(hidden_in, "src", axis=1, tiled=True)
    source = gathered.astype(jnp.float32)
    spread = jnp.mean(source * source, axis=-1, keepdims=True)
    normed = (source * lax.rsqrt(spread + 1e-06) * norm_gain.astype(jnp.float32)).astype(
        jnp.bfloat16
    )
    queries = jnp.dot(normed, w_query, preferred_element_type=jnp.float32).astype(jnp.bfloat16)
    tok_rows = queries.shape[0]
    heads_here = queries.shape[1] // HD
    keys_here = keys_cache.shape[0]
    tgt_count = lax.axis_size("tgt")
    slot_size = keys_here * tgt_count // lengths.shape[0]
    queries3 = queries.reshape(tok_rows, heads_here, HD)
    running = start_state(heads_here, tok_rows)
    offset = jnp.int32(0)
    key_part = lax.all_gather(keys_cache, "tgt", axis=0, tiled=True)
    value_part = lax.all_gather(values_cache, "tgt", axis=0, tiled=True)
    count = key_part.shape[0]
    keys3 = key_part.reshape(count, heads_here, HD)
    values3 = value_part.reshape(count, heads_here, HD)
    for begin in range(0, count, 512):
        finish = min(begin + 512, count)
        allowed = allowed_rows(offset + begin, finish - begin, lengths, slot_size)
        key_block = keys3[begin:finish]
        value_block = values3[begin:finish]
        running = absorb(running, queries3, key_block, value_block, allowed)
    best, total, accum = running
    normalized = accum / total.T[:, :, None]
    attended = normalized.reshape(tok_rows, heads_here * HD).astype(jnp.bfloat16)
    branch = jnp.dot(
        lax.all_gather(attended, "src", axis=1, tiled=True),
        w_output,
        preferred_element_type=jnp.float32,
    )
    return hidden_in.astype(jnp.float32) + branch


def solution(mesh):
    in_specs = (
        P("tgt", "src"),
        P(),
        P(None, "src"),
        P("tgt", "src"),
        P("tgt", "src"),
        P(),
        P(None, "src"),
    )
    out_specs = P("tgt", "src")
    return jax.shard_map(body, mesh=mesh, in_specs=in_specs, out_specs=out_specs, check_vma=False)
```

profile of v0, /device:TPU:2, one launch (start us, length us, event | category | flops | bytes accessed | tf_op | source)
XLA Modules:
  0.0 399.4 jit_solution(5198957430856353362)
XLA Ops:
  6.5 0.7 all-gather.5.cloned.1.call-update
  7.3 0.7 all-gather.7.cloned.1.call-update
  8.1 0.7 all-gather.9.cloned.1.call-update
  8.8 0.7 convert_element_type.47
  9.6 0.8 select_reduce_fusion
  10.9 0.6 fusion.107
  11.5 109.4 %all-gather.5.cloned.1.call-done = bf16[256,4096]{1,0:T(8,128)(2,1)} async-done(((bf16[256,256]{1,0:T(8,128)(2,1)}), bf16[256,4096]{1,0:T(8,128)(2,1)}) %all-gather.5.cloned.1.call-update) | async-done | bytes 2097168 | tf_op jit(solution)/shard_map/all_gather | solution.py:47
  120.9 2.2 fusion
  123.2 1.2 fusion.48
  124.4 54.7 %all-gather.7.cloned.1.call-done = bf16[4096,256]{1,0:T(8,128)(2,1)} async-done(((bf16[128,256]{1,0:T(8,128)(2,1)}), bf16[4096,256]{1,0:T(8,128)(2,1)}) %all-gather.7.cloned.1.call-update) | async-done | bytes 2097168 | tf_op jit(solution)/shard_map/all_gather | solution.py:62
  179.1 2.4 fusion.165
  181.5 1.8 copy.24
  183.4 59.8 %all-gather.9.cloned.1.call-done = bf16[4096,256]{1,0:T(8,128)(2,1)} async-done(((bf16[128,256]{1,0:T(8,128)(2,1)}), bf16[4096,256]{1,0:T(8,128)(2,1)}) %all-gather.9.cloned.1.call-update) | async-done | bytes 2097168 | tf_op jit(solution)/shard_map/all_gather | solution.py:63
  243.2 2.8 fusion.164
  246.0 1.8 copy.25
  247.8 1.8 copy.39
  249.6 1.8 copy.37
  251.3 1.8 copy.35
  253.1 1.8 copy.33
  254.9 1.8 copy.31
  256.8 1.8 copy.29
  258.6 1.8 copy.27
  260.4 1.8 copy.38
  262.2 1.8 copy.36
  264.0 0.8 copy.34
  265.4 0.6 fusion.8
  267.8 0.6 fusion.12
  268.4 0.6 fusion.13
  268.9 0.6 fusion.14
  269.5 0.6 fusion.7
  270.2 0.6 fusion.29
  270.8 0.7 convolution_bitcast_fusion
  271.5 0.6 fusion.27
  272.4 0.7 convolution_bitcast_fusion.1
  273.1 0.6 fusion.25
  274.0 0.7 convolution_bitcast_fusion.2
  274.7 0.8 fusion.23
  275.6 0.7 convolution_bitcast_fusion.3
  276.3 0.6 fusion.21
  277.2 0.7 convolution_bitcast_fusion.4
  277.9 0.6 fusion.19
  278.8 0.7 convolution_bitcast_fusion.5
  279.5 0.6 fusion.17
  280.5 0.6 convolution_bitcast_fusion.6
  281.1 0.6 fusion.15
  282.1 1.4 fusion.47
  283.5 105.7 %all-gather.11.cloned.1.call-done = bf16[256,4096]{0,1:T(8,128)(2,1)} async-done(((bf16[256,256]{0,1:T(8,128)(2,1)}), bf16[256,4096]{0,1:T(8,128)(2,1)}) %all-gather.11.cloned.1.call-update) | async-done | bytes 2097168 | tf_op jit(solution)/shard_map/all_gather | solution.py:77
  389.2 3.7 convolution_add_fusion
  (65 shorter events, 5.1 us)
Async XLA Ops:
  6.5 116.6 %copy-start = (bf16[4096,256]{1,0:T(8,128)(2,1)S(1)}, bf16[4096,256]{1,0:T(8,128)(2,1)}, u32[]{:S(2)}) copy-start(bf16[4096,256]{1,0:T(8,128)(2,1)} %param.9) | copy-start | bytes 6291460
  6.5 114.4 %all-gather.5.cloned.1.call-start = ((), (), s32[]{:S(2)}) async-start(), calls=%async_computation | async-start | bytes 2228224 | tf_op jit(solution)/shard_map/all_gather | solution.py:47
  7.3 171.9 %all-gather.7.cloned.1.call-start = ((), (), s32[]{:S(2)}) async-start(), calls=%async_computation.1 | async-start | bytes 2162688 | tf_op jit(solution)/shard_map/all_gather | solution.py:62
  8.0 235.1 %all-gather.9.cloned.1.call-start = ((), (), s32[]{:S(2)}) async-start(), calls=%async_computation.2 | async-start | bytes 2162688 | tf_op jit(solution)/shard_map/all_gather | solution.py:63
  8.7 380.5 %all-gather.11.cloned.1.call-start = ((), (), s32[]{:S(2)}) async-start(), calls=%async_computation.3 | async-start | bytes 2228224 | tf_op jit(solution)/shard_map/all_gather | solution.py:77
  120.9 2.3 copy-start.1
  266.0 1.2 copy-start.16
  266.5 1.2 copy-start.5
  266.5 1.2 copy-start.18
  267.1 1.2 copy-start.4
  267.1 1.2 copy-start.15
  267.7 1.2 copy-start.3
  267.7 1.2 copy-start.17
  268.3 1.2 copy-start.2
  269.5 1.3 copy-start.13
  271.5 1.0 copy-start.12
  273.1 1.0 copy-start.11
  274.7 1.0 copy-start.10
  276.3 1.0 copy-start.9
  277.9 1.0 copy-start.8
  279.5 1.0 copy-start.7
  281.1 1.0 copy-start.6
  282.1 107.2 %copy-start.14 = (bf16[256,256]{1,0:T(8,128)(2,1)S(1)}, bf16[256,256]{1,0:T(8,128)(2,1)}, u32[]{:S(2)}) copy-start(bf16[256,256]{1,0:T(8,128)(2,1)} %param.7) | copy-start | bytes 393220
Sparse Core Ops, SparseCore 0:
  10.4 110.4 all-gather.4
  123.1 56.0 all-gather.6
  181.3 61.8 all-gather.8
  283.6 105.5 all-gather.10
where the time goes:
time: 400 us; the launch traced here: 399 us
  waiting for transfers between devices  332 us (83%)
  local copies, waits for them, and re-layouts  28.4 us (7%)
  matrix products  15.4 us (4%)
  between operations  13.4 us (3%)
  other arithmetic  10.3 us (3%)
    all_gather x1, waiting for transfers between devices, body(): gathered = lax.all_gather(hidden_in, 'src', axis=1, tiled=True)  109 us
    all_gather x1, waiting for transfers between devices, body(): lax.all_gather(attended, 'src', axis=1, tiled=True)  106 us
    all_gather x1, waiting for transfers between devices, body(): value_part = lax.all_gather(values_cache, 'tgt', axis=0, tiled=True)  59.8 us
    all_gather x1, waiting for transfers between devices, body(): key_part = lax.all_gather(keys_cache, 'tgt', axis=0, tiled=True)  54.7 us
    slice x9, local copies, waits for them, and re-layouts, body(): value_block = values3[begin:finish]  17.2 us
    slice x9, local copies, waits for them, and re-layouts, body(): key_block = keys3[begin:finish]  9.23 us
  transfers between devices with their start and end apart: 4, of which 4 were waited for; matrix products, arithmetic and copies ran while one was open for 3% of the time, Pallas kernels for 0%

commit v1 on v0

v1 whole, which is shorter than its diff:
```python
import functools

import jax
import jax.numpy as jnp
from jax import lax
from jax.experimental import pallas as pl
from jax.experimental.pallas import tpu as pltpu
from jax.sharding import PartitionSpec as P

MESH = pl.DeviceIdType.MESH
HD = 64
NZ, NX, NYL = 8, 4, 4
SRC, TGT = 16, 32
TOK, FEAT, POS, WIDE = 256, 256, 128, 4096
PAIR = 128
BLK = 512
NB = WIDE // BLK
SCALE = HD ** -0.5 * 1.4426950408889634
F32, BF16 = jnp.float32, jnp.bfloat16
NT = (((1,), (1,)), ((), ()))


def kernel(
    hid_hbm, gain_ref, wq_hbm, keys_hbm, vals_hbm, len_ref, wo_hbm, out_ref,
    hbuf, kv, kc, vp, wq, wo, abuf, sbuf, mbuf, obuf, qacc, ssq, qm, krow,
    loc_sem, h_send, h_recv, a_send, a_recv, kv_send, kv_recv, kk_recv, vv_recv,
):
    src = lax.axis_index("src")
    tgt = lax.axis_index("tgt")
    z, yh = src // 2, src % 2
    x, yl, core = tgt // 8, (tgt // 2) % 4, tgt % 2
    partner = z * 2 + (1 - yh)
    z_right = ((z + 1) % NZ) * 2 + yh
    z_left = ((z + NZ - 1) % NZ) * 2 + yh
    sib = x * 8 + yl * 2 + (1 - core)

    def at_tgt(xx, yy):
        return (xx % NX) * 8 + (yy % NYL) * 2 + core

    x_right, x_left = at_tgt(x + 1, yl), at_tgt(x + NX - 1, yl)

    loads = [
        pltpu.make_async_copy(hid_hbm, hbuf.at[src], loc_sem.at[0]),
        pltpu.make_async_copy(keys_hbm, kv.at[tgt, 0], loc_sem.at[1]),
        pltpu.make_async_copy(vals_hbm, kv.at[tgt, 1], loc_sem.at[2]),
        pltpu.make_async_copy(wq_hbm, wq, loc_sem.at[3]),
        pltpu.make_async_copy(wo_hbm, wo, loc_sem.at[4]),
    ]
    for c in loads:
        c.start()

    barrier = pltpu.get_barrier_semaphore()
    friends = [
        (partner, tgt), (z_right, tgt), (z_left, tgt),
        (src, x_right), (src, x_left), (src, sib),
        (src, at_tgt(x, yl + 1)), (src, at_tgt(x, yl + 2)), (src, at_tgt(x, yl + 3)),
    ]
    for f in friends:
        pl.semaphore_signal(barrier, inc=1, device_id=f, device_id_type=MESH)

    qacc[...] = jnp.zeros_like(qacc)
    ssq[...] = jnp.zeros_like(ssq)
    for c in loads[:3]:
        c.wait()
    pl.semaphore_wait(barrier, len(friends))

    pending = []

    def send(ref, ssem, rsem, dev):
        c = pltpu.make_async_remote_copy(
            src_ref=ref, dst_ref=ref, send_sem=ssem, recv_sem=rsem,
            device_id=dev, device_id_type=MESH,
        )
        c.start()
        pending.append(c)

    def arrived(ref, rsem):
        pltpu.make_async_remote_copy(
            src_ref=ref, dst_ref=ref, send_sem=rsem, recv_sem=rsem,
            device_id=(src, sib), device_id_type=MESH,
        ).wait_recv()

    def owner_of(col, dist, way):
        zz = (z - dist + NZ) % NZ if way == "R" else (z + dist) % NZ
        return zz * 2 + (yh if col == 0 else 1 - yh)

    class Ring:
        def __init__(self, slot, ssem, rsem):
            self.slot, self.ssem, self.rsem, self.count = slot, ssem, rsem, 0

        def push(self, owner, half, dev):
            send(self.slot(owner, half), self.ssem.at[self.count], self.rsem.at[owner * 2 + half], dev)
            self.count += 1

        def own(self, half):
            self.push(src, half, (z_right, tgt))
            self.push(src, half, (z_left, tgt))
            self.push(src, half, (partner, tgt))

        def take(self, col, dist, way, half):
            owner = owner_of(col, dist, way)
            arrived(self.slot(owner, half), self.rsem.at[owner * 2 + half])
            last = {("R", 0): 3, ("R", 1): 2, ("L", 0): 2, ("L", 1): 3}[(way, col)]
            if dist <= last:
                self.push(owner, half, (z_right if way == "R" else z_left, tgt))
            return owner

        def both(self, col, dist, half):
            ways = "RL" if dist < 4 else ("R" if col == 0 else "L")
            return [self.take(col, dist, way, half) for way in ways]

        def cross(self, half):
            arrived(self.slot(partner, half), self.rsem.at[partner * 2 + half])
            self.push(partner, half, (z_right, tgt))
            self.push(partner, half, (z_left, tgt))

    hid = Ring(lambda o, h: hbuf.at[o, pl.ds(h * 128, 128)], h_send, h_recv)
    att = Ring(lambda o, h: abuf.at[o, h], a_send, a_recv)
    kv_count = [0]

    def kv_push(ref, rsem, dev):
        send(ref, kv_send.at[kv_count[0]], rsem, dev)
        kv_count[0] += 1

    def to_sibling(s):
        kv_push(kv.at[s], kv_recv.at[s], (src, sib))

    def q_part(owner):
        h = hbuf[owner].astype(F32)
        sq = h * h
        ssq[...] += sq[:, :128] + sq[:, 128:]
        hg = (h * gain_ref[owner]).astype(BF16)
        w = wq[pl.ds(pl.multiple_of(owner * FEAT, FEAT), FEAT), :]
        qacc[...] += jnp.dot(hg, w, preferred_element_type=F32)

    def prep(s):
        limit = len_ref[s // 2] - (s % 2) * POS
        rows = lax.broadcasted_iota(jnp.int32, (POS, FEAT), 0)
        at = pl.ds(pl.multiple_of(s * POS, POS), POS)
        k = kv[s, 0].astype(F32)
        kc[at, :] = jnp.where(rows < limit, k, krow[0:1, :]).astype(BF16)
        v = kv[s, 1].astype(F32)
        ok = rows[:, :PAIR] < limit
        low = lax.broadcasted_iota(jnp.int32, (POS, PAIR), 1) < HD
        for p in range(2):
            vv = v[:, p * PAIR:(p + 1) * PAIR]
            vp[2 * p, at, :] = jnp.where(ok, jnp.where(low, vv, 1.0), 0.0).astype(BF16)
            vp[2 * p + 1, at, :] = jnp.where(ok, jnp.where(low, 1.0, vv), 0.0).astype(BF16)

    for half in range(2):
        hid.own(half)
    kv_push(kv.at[tgt], kv_recv.at[tgt], (src, x_right))
    kv_push(kv.at[tgt], kv_recv.at[tgt], (src, x_left))
    to_sibling(tgt)
    for k in (1, 3, 2):
        kv_push(kv.at[tgt], kv_recv.at[tgt], (src, at_tgt(x, yl + k)))

    loads[3].wait()
    q_part(src)

    def y_take(k):
        s = at_tgt(x, yl + k)
        arrived(kv.at[s], kv_recv.at[s])
        kv_push(kv.at[s], kv_recv.at[s], (src, x_right))
        kv_push(kv.at[s], kv_recv.at[s], (src, x_left))
        to_sibling(s)
        return s

    def x_take(k):
        s_left, s_right = at_tgt(x + NX - 1, yl + k), at_tgt(x + 1, yl + k)
        arrived(kv.at[s_left], kv_recv.at[s_left])
        kv_push(kv.at[s_left, 0], kk_recv.at[s_left], (src, x_right))
        arrived(kv.at[s_right], kv_recv.at[s_right])
        kv_push(kv.at[s_right, 1], vv_recv.at[s_right], (src, x_left))
        to_sibling(s_left)
        to_sibling(s_right)
        return s_left, s_right

    def far_take(k):
        s = at_tgt(x + 2, yl + k)
        arrived(kv.at[s, 0], kk_recv.at[s])
        arrived(kv.at[s, 1], vv_recv.at[s])
        to_sibling(s)
        return s

    def sib_of(s):
        return s + 1 - 2 * core

    def sib_take(s):
        o = sib_of(s)
        arrived(kv.at[o], kv_recv.at[o])
        return o

    hid.both(0, 1, 0)
    for o in hid.both(0, 1, 1):
        q_part(o)
    s_l0, s_r0 = x_take(0)
    o = sib_take(tgt)
    krow[...] = jnp.broadcast_to(
        kv[x * 8 + yl * 2, 0, 0:16, :].astype(F32)[0:1, :], krow.shape
    )
    prep(tgt)
    prep(o)
    hid.both(0, 2, 0)
    s_y1 = y_take(1)
    prep(s_l0)
    prep(s_r0)
    for o in hid.both(0, 2, 1):
        q_part(o)
    s_f0 = far_take(0)
    s_y3 = y_take(3)
    prep(s_y1)
    hid.cross(0)
    hid.cross(1)
    hid.both(0, 3, 0)
    q_part(partner)
    s_y2 = y_take(2)
    prep(s_f0)
    prep(s_y3)
    for o in hid.both(0, 3, 1):
        q_part(o)
    s_l1, s_r1 = x_take(1)
    prep(s_y2)
    prep(sib_take(s_l0))
    prep(sib_take(s_r0))
    hid.both(0, 4, 0)
    hid.both(1, 1, 0)
    prep(sib_take(s_y1))
    prep(sib_take(s_f0))
    for o in hid.both(0, 4, 1) + hid.both(1, 1, 1):
        q_part(o)
    s_f1 = far_take(1)
    s_l3, s_r3 = x_take(3)
    prep(s_l1)
    prep(s_r1)
    prep(sib_take(s_y3))
    hid.both(1, 2, 0)
    prep(s_f1)
    prep(s_l3)
    prep(s_r3)
    prep(sib_take(s_y2))
    for o in hid.both(1, 2, 1):
        q_part(o)
    s_f3 = far_take(3)
    prep(sib_take(s_l1))
    prep(sib_take(s_r1))
    s_l2, s_r2 = x_take(2)
    prep(s_f3)
    prep(sib_take(s_f1))
    hid.both(1, 3, 0)
    prep(s_l2)
    prep(s_r2)
    prep(sib_take(s_l3))
    prep(sib_take(s_r3))
    for o in hid.both(1, 3, 1):
        q_part(o)
    hid.both(1, 4, 0)
    s_f2 = far_take(2)
    prep(s_f2)
    prep(sib_take(s_f3))
    prep(sib_take(s_l2))
    prep(sib_take(s_r2))
    for o in hid.both(1, 4, 1):
        q_part(o)
    prep(sib_take(s_f2))

    mean = jnp.sum(ssq[...], axis=1, keepdims=True) / WIDE
    q = qacc[...] * (lax.rsqrt(mean + 1e-06) * SCALE)
    lane_low = lax.broadcasted_iota(jnp.int32, (TOK, PAIR), 1) < HD
    for p in range(2):
        qp = q[:, p * PAIR:(p + 1) * PAIR]
        qm[2 * p] = jnp.where(lane_low, qp, 0.0).astype(BF16)
        qm[2 * p + 1] = jnp.where(lane_low, 0.0, qp).astype(BF16)

    def scores(h, j):
        at = pl.ds(pl.multiple_of(j * BLK, BLK), BLK)
        cols = slice((h // 2) * PAIR, (h // 2 + 1) * PAIR)
        s = lax.dot_general(qm[h], kc[at, cols], NT, preferred_element_type=F32)
        sbuf[h % 2, j] = s
        m = s[:, :PAIR]
        for i in range(1, BLK // PAIR):
            m = jnp.maximum(m, s[:, i * PAIR:(i + 1) * PAIR])
        mbuf[h % 2] = jnp.maximum(mbuf[h % 2], m)

    def weigh(h, j):
        at = pl.ds(pl.multiple_of(j * BLK, BLK), BLK)
        top = mbuf[2 + h % 2]
        e = [
            jnp.exp2(sbuf[h % 2, j, :, i * PAIR:(i + 1) * PAIR] - top).astype(BF16)
            for i in range(BLK // PAIR)
        ]
        e = jnp.concatenate(e, axis=1)
        obuf[h % 2] += jnp.dot(e, vp[h, at, :], preferred_element_type=F32)

    def clear(h):
        mbuf[h % 2] = jnp.full((TOK, PAIR), -3e38, F32)

    def settle(h):
        mbuf[2 + h % 2] = jnp.broadcast_to(
            jnp.max(mbuf[h % 2], axis=1, keepdims=True), (TOK, PAIR)
        )
        obuf[h % 2] = jnp.zeros((TOK, PAIR), F32)

    def stage(h_weigh, h_score):
        if h_score is not None:
            clear(h_score)

        def step(j, carry):
            if h_score is not None:
                scores(h_score, j)
            if h_weigh is not None:
                weigh(h_weigh, j)
            return carry

        lax.fori_loop(0, NB, step, 0)
        if h_score is not None:
            settle(h_score)

    def finish(p):
        top = jnp.where(lane_low, obuf[0], obuf[1])
        low = jnp.where(lane_low, obuf[1], obuf[0])
        abuf[src, p] = (top / pltpu.roll(low, HD, 1)).astype(BF16)

    def o_part(owner, p):
        w = wo[pl.ds(pl.multiple_of(owner * FEAT + p * PAIR, PAIR), PAIR), :]
        qacc[...] += jnp.dot(abuf[owner, p], w, preferred_element_type=F32)

    stage(None, 0)
    stage(0, 1)
    stage(1, None)
    finish(0)
    att.own(0)
    loads[4].wait()
    qacc[...] = jnp.zeros_like(qacc)
    o_part(src, 0)
    stage(None, 2)
    done = [(o, 0) for o in att.both(0, 1, 0)]
    stage(2, 3)
    done += [(o, 0) for o in att.both(0, 2, 0)]
    stage(3, None)
    finish(1)
    att.own(1)

    def flush():
        for o, p in done:
            o_part(o, p)
        done.clear()

    att.cross(0)
    done += [(o, 0) for o in att.both(0, 3, 0)]
    done += [(src, 1), (partner, 0)]
    flush()
    for step in (
        (0, 1, 1), (1, 1, 0), (0, 2, 1), (0, 4, 0), None, (0, 3, 1), (1, 2, 0),
        (1, 1, 1), (0, 4, 1), (1, 3, 0), (1, 2, 1), (1, 4, 0), (1, 3, 1), (1, 4, 1),
    ):
        if step is None:
            att.cross(1)
            done.append((partner, 1))
        else:
            col, dist, half = step
            done += [(o, half) for o in att.both(col, dist, half)]
        flush()

    out_ref[...] = qacc[...]
    for c in pending:
        c.wait_send()


def body(hidden_in, norm_gain, w_query, keys_cache, values_cache, lengths, w_output):
    gain = norm_gain.astype(F32).reshape(SRC, 1, FEAT)
    anywhere = pl.BlockSpec(memory_space=pl.ANY)
    vmem = pl.BlockSpec(memory_space=pltpu.VMEM)
    smem = pl.BlockSpec(memory_space=pltpu.SMEM)
    dma = pltpu.SemaphoreType.DMA
    branch = pl.pallas_call(
        kernel,
        out_shape=jax.ShapeDtypeStruct((TOK, FEAT), F32),
        in_specs=[anywhere, vmem, anywhere, anywhere, anywhere, smem, anywhere],
        out_specs=vmem,
        scratch_shapes=[
            pltpu.VMEM((SRC, TOK, FEAT), BF16),
            pltpu.VMEM((TGT, 2, POS, FEAT), BF16),
            pltpu.VMEM((WIDE, FEAT), BF16),
            pltpu.VMEM((4, WIDE, PAIR), BF16),
            pltpu.VMEM((WIDE, FEAT), BF16),
            pltpu.VMEM((WIDE, FEAT), BF16),
            pltpu.VMEM((SRC, 2, TOK, PAIR), BF16),
            pltpu.VMEM((2, NB, TOK, BLK), F32),
            pltpu.VMEM((4, TOK, PAIR), F32),
            pltpu.VMEM((2, TOK, PAIR), F32),
            pltpu.VMEM((TOK, FEAT), F32),
            pltpu.VMEM((TOK, PAIR), F32),
            pltpu.VMEM((4, TOK, PAIR), BF16),
            pltpu.VMEM((8, FEAT), F32),
            dma((5,)),
            dma((32,)), dma((32,)),
            dma((32,)), dma((32,)),
            dma((40,)), dma((32,)), dma((32,)), dma((32,)),
        ],
        compiler_params=pltpu.CompilerParams(
            collective_id=0, has_side_effects=True, vmem_limit_bytes=52 * 1024 * 1024,
        ),
        cost_estimate=pl.CostEstimate(
            flops=6_000_000_000, bytes_accessed=8_000_000, transcendentals=4_200_000
        ),
    )(hidden_in, gain, w_query, keys_cache, values_cache, lengths, w_output)
    return hidden_in.astype(F32) + branch


def solution(mesh):
    in_specs = (
        P("tgt", "src"),
        P(),
        P(None, "src"),
        P("tgt", "src"),
        P("tgt", "src"),
        P(),
        P(None, "src"),
    )
    out_specs = P("tgt", "src")
    return jax.shard_map(body, mesh=mesh, in_specs=in_specs, out_specs=out_specs, check_vma=False)
```

time: 400 us -> 97.4 us (0.24)
  the two profiles are of different devices: /device:TPU:2 before, /device:TPU:8 now
where the time goes in v1:
time: 97.4 us; the launch traced here: 97.2 us
  Pallas kernels  92.5 us (95%)
  local copies, waits for them, and re-layouts  3.24 us (3%)
  other arithmetic  1.43 us (1%)
    pallas_call x1, Pallas kernels, body(): pl.pallas_call(kernel, out_shape=jax.ShapeDtypeStruct((TOK, FEAT), F32),...  92.5 us
    unnamed x8, local copies, waits for them, and re-layouts  3.24 us

profile of v1, /device:TPU:8, one launch (start us, length us, event | category | flops | bytes accessed | tf_op | source)
XLA Modules:
  0.0 97.2 jit_solution(9389430906238923057)
XLA Ops:
  0.0 0.7 reshape.7
  0.7 0.0 copy-start
  0.7 0.9 copy-done
  1.6 0.0 copy-start.1
  1.6 0.8 copy-done.1
  2.4 0.0 copy-start.2
  2.4 0.8 copy-done.2
  3.3 0.0 copy-start.3
  3.3 0.7 copy-done.3
  3.9 92.5 %shard_map.73 = f32[256,256]{1,0:T(8,128)S(1)} custom-call(bf16[256,256]{1,0:T(8,128)(2,1)S(1)} %copy-done, f32[16,1,256]{2,1,0:T(1,128)S(1)} %bitcast.1, bf16[4096,256]{1,0:T(8,128)(2,1)} %wq_hbm.1, bf16[128,256]{1,0:T(8,128)(2,1)S(1)} %copy-done.1, bf16[128,256]{1,0:T(8,128)(2,1)S(1)} %copy-done.2, s32[16]{0:T(128)S(1)} %copy-done.3, bf16[4096,256]{1,0:T(8,128)(2,1)} %wo_hbm.1), custom_call_target="tpu_custom_call" | custom-call | flops 6000000000 | bytes 8000000 | tf_op jit(solution)/shard_map/pallas_call | solution.py:376
  96.4 0.7 convert_add_fusion
Async XLA Ops:
  0.7 0.9 copy-start
  1.6 0.8 copy-start.1
  2.4 0.8 copy-start.2
  3.3 0.7 copy-start.3

commit v2 on v1

v2 whole, which is shorter than its diff:
```python
import functools

import jax
import jax.numpy as jnp
from jax import lax
from jax.experimental import pallas as pl
from jax.experimental.pallas import tpu as pltpu
from jax.sharding import PartitionSpec as P

MESH = pl.DeviceIdType.MESH
HD = 64
NZ, NX, NYL = 8, 4, 4
SRC, TGT = 16, 32
TOK, FEAT, POS, WIDE = 256, 256, 128, 4096
PAIR = 128
HALF = 128
BLK = 512
NB = WIDE // BLK
SCALE = HD ** -0.5 * 1.4426950408889634
F32, BF16 = jnp.float32, jnp.bfloat16
NT = (((1,), (1,)), ((), ()))


def kernel(
    hid_hbm, gain_ref, wq_hbm, keys_hbm, vals_hbm, len_ref, wo_hbm, out_ref,
    hbuf, kv, kc, vp, wq, wo, abuf, sbuf, mbuf, obuf, qacc, ssq, qm, krow,
    loc_sem, h_send, h_recv, a_send, a_recv, kv_send, kv_recv,
):
    src = lax.axis_index("src")
    tgt = lax.axis_index("tgt")
    z, yh = src // 2, src % 2
    x, yl, core = tgt // 8, (tgt // 2) % 4, tgt % 2
    partner = z * 2 + (1 - yh)
    z_right = ((z + 1) % NZ) * 2 + yh
    z_left = ((z + NZ - 1) % NZ) * 2 + yh
    sib = x * 8 + yl * 2 + (1 - core)

    def at_tgt(xx, yy):
        return (xx % NX) * 8 + (yy % NYL) * 2 + core

    x_right, x_left = at_tgt(x + 1, yl), at_tgt(x + NX - 1, yl)

    loads = [
        pltpu.make_async_copy(hid_hbm, hbuf.at[src], loc_sem.at[0]),
        pltpu.make_async_copy(keys_hbm, kv.at[tgt, 0], loc_sem.at[1]),
        pltpu.make_async_copy(vals_hbm, kv.at[tgt, 1], loc_sem.at[2]),
        pltpu.make_async_copy(wq_hbm, wq, loc_sem.at[3]),
        pltpu.make_async_copy(wo_hbm, wo, loc_sem.at[4]),
    ]
    for c in loads:
        c.start()

    barrier = pltpu.get_barrier_semaphore()
    friends = [
        (partner, tgt), (z_right, tgt), (z_left, tgt),
        (src, x_right), (src, x_left), (src, sib),
        (src, at_tgt(x, yl + 1)), (src, at_tgt(x, yl + 2)), (src, at_tgt(x, yl + 3)),
    ]
    for f in friends:
        pl.semaphore_signal(barrier, inc=1, device_id=f, device_id_type=MESH)

    qacc[...] = jnp.zeros_like(qacc)
    ssq[...] = jnp.zeros_like(ssq)
    for c in loads[:3]:
        c.wait()
    pl.semaphore_wait(barrier, len(friends))

    pending = []

    def send(ref, ssem, rsem, dev):
        c = pltpu.make_async_remote_copy(
            src_ref=ref, dst_ref=ref, send_sem=ssem, recv_sem=rsem,
            device_id=dev, device_id_type=MESH,
        )
        c.start()
        pending.append(c)

    def arrived(ref, rsem):
        pltpu.make_async_remote_copy(
            src_ref=ref, dst_ref=ref, send_sem=rsem, recv_sem=rsem,
            device_id=(src, sib), device_id_type=MESH,
        ).wait_recv()

    def owner_of(col, dist, way):
        zz = (z - dist + NZ) % NZ if way == "R" else (z + dist) % NZ
        return zz * 2 + (yh if col == 0 else 1 - yh)

    class Ring:
        def __init__(self, slot, ssem, rsem):
            self.slot, self.ssem, self.rsem, self.count = slot, ssem, rsem, 0

        def push(self, owner, half, dev):
            send(self.slot(owner, half), self.ssem.at[self.count], self.rsem.at[owner * 2 + half], dev)
            self.count += 1

        def own(self, half):
            self.push(src, half, (z_right, tgt))
            self.push(src, half, (z_left, tgt))
            self.push(src, half, (partner, tgt))

        def take(self, col, dist, way, half):
            owner = owner_of(col, dist, way)
            arrived(self.slot(owner, half), self.rsem.at[owner * 2 + half])
            last = {("R", 0): 3, ("R", 1): 2, ("L", 0): 2, ("L", 1): 3}[(way, col)]
            if dist <= last:
                self.push(owner, half, (z_right if way == "R" else z_left, tgt))
            return owner

        def both(self, col, dist, half):
            ways = "RL" if dist < 4 else ("R" if col == 0 else "L")
            return [self.take(col, dist, way, half) for way in ways]

        def cross(self, half):
            arrived(self.slot(partner, half), self.rsem.at[partner * 2 + half])
            self.push(partner, half, (z_right, tgt))
            self.push(partner, half, (z_left, tgt))

    hid = Ring(lambda o, h: hbuf.at[o, pl.ds(h * HALF, HALF)], h_send, h_recv)
    att = Ring(lambda o, h: abuf.at[o, pl.ds(h * HALF, HALF)], a_send, a_recv)
    kv_count = [0]

    def kv_push(s, u, dev):
        send(kv.at[s, u], kv_send.at[kv_count[0]], kv_recv.at[s * 2 + u], dev)
        kv_count[0] += 1

    def kv_wait(s, u):
        arrived(kv.at[s, u], kv_recv.at[s * 2 + u])

    def q_part(owner):
        h = hbuf[owner].astype(F32)
        sq = h * h
        ssq[...] += sq[:, :PAIR] + sq[:, PAIR:]
        hg = (h * gain_ref[owner]).astype(BF16)
        w = wq[pl.ds(pl.multiple_of(owner * FEAT, FEAT), FEAT), :]
        qacc[...] += jnp.dot(hg, w, preferred_element_type=F32)

    def prep(s, u):
        limit = len_ref[s // 2] - (s % 2) * POS
        ok = lax.broadcasted_iota(jnp.int32, (POS, FEAT), 0) < limit
        at = pl.ds(pl.multiple_of(s * POS, POS), POS)
        data = kv[s, u].astype(F32)
        if u == 0:
            kc[at, :] = jnp.where(ok, data, krow[0:1, :]).astype(BF16)
        else:
            data = jnp.where(ok, data, 0.0).astype(BF16)
            mask = jnp.where(ok[:, :PAIR], 1.0, 0.0).astype(BF16)
            for p in range(2):
                vp[p, at, :PAIR] = data[:, p * PAIR:(p + 1) * PAIR]
                vp[p, at, PAIR:] = mask

    for half in range(2):
        hid.own(half)
    for u in range(2):
        kv_push(tgt, u, (src, x_right))
        kv_push(tgt, u, (src, x_left))
        for k in (1, 3, 2):
            kv_push(tgt, u, (src, at_tgt(x, yl + k)))
        kv_push(tgt, u, (src, sib))

    loads[3].wait()
    q_part(src)

    backlog = []

    def own_taken(s, u):
        kv_push(s, u, (src, sib))
        prep(s, u)
        backlog.append((s + 1 - 2 * core, u))

    def take_y(k, u):
        s = at_tgt(x, yl + k)
        kv_wait(s, u)
        kv_push(s, u, (src, x_right))
        kv_push(s, u, (src, x_left))
        own_taken(s, u)

    def take_x(k, u):
        s_left, s_right = at_tgt(x + NX - 1, yl + k), at_tgt(x + 1, yl + k)
        kv_wait(s_left, u)
        if u == 0:
            kv_push(s_left, u, (src, x_right))
        kv_wait(s_right, u)
        if u == 1:
            kv_push(s_right, u, (src, x_left))
        own_taken(s_left, u)
        own_taken(s_right, u)

    def take_far(k, u):
        s = at_tgt(x + 2, yl + k)
        kv_wait(s, u)
        own_taken(s, u)

    def drain(keep):
        while len(backlog) > keep:
            s, u = backlog.pop(0)
            kv_wait(s, u)
            prep(s, u)

    def first_row():
        other = tgt + 1 - 2 * core
        kv_wait(other, 0)
        even = kv[x * 8 + yl * 2, 0, 0:16, :].astype(F32)[0:1, :]
        krow[...] = jnp.broadcast_to(even, krow.shape)
        prep(tgt, 0)
        prep(tgt, 1)
        prep(other, 0)
        backlog.append((other, 1))

    def take_z(col, dist, half):
        owners = hid.both(col, dist, half)
        if half == 1:
            for o in owners:
                q_part(o)

    def cross_z():
        hid.cross(0)
        hid.cross(1)

    def cross_q():
        q_part(partner)

    Z, Y, X, W = take_z, take_y, take_x, take_far
    for event in (
        (Z, 0, 1, 0), (first_row,), (X, 0, 0), (Z, 0, 1, 1), (Y, 1, 0), (X, 0, 1),
        (Y, 3, 0), (cross_z,), (Z, 0, 2, 0), (W, 0, 0), (cross_q,), (Z, 1, 1, 0), (Y, 2, 0),
        (X, 1, 0), (Z, 0, 2, 1), (W, 0, 1), (Y, 1, 1), (Z, 1, 1, 1), (X, 3, 0),
        (W, 1, 0), (Z, 0, 3, 0), (Y, 3, 1), (X, 2, 0), (Z, 1, 2, 0), (W, 3, 0),
        (Z, 0, 3, 1), (X, 1, 1), (Y, 2, 1), (Z, 1, 2, 1), (W, 2, 0), (Z, 0, 4, 0),
        (W, 1, 1), (X, 3, 1), (Z, 1, 3, 0), (Z, 0, 4, 1), (X, 2, 1), (W, 3, 1),
        (Z, 1, 3, 1), (Z, 1, 4, 0), (W, 2, 1), (Z, 1, 4, 1),
    ):
        event[0](*event[1:])
        drain(4)
    drain(0)

    mean = jnp.sum(ssq[...], axis=1, keepdims=True) / WIDE
    q = qacc[...] * (lax.rsqrt(mean + 1e-06) * SCALE)
    low = lax.broadcasted_iota(jnp.int32, (HALF, PAIR), 1) < HD
    for t in range(2):
        for p in range(2):
            qp = q[t * HALF:(t + 1) * HALF, p * PAIR:(p + 1) * PAIR]
            qm[2 * t + p, :HALF] = jnp.where(low, qp, 0.0).astype(BF16)
            qm[2 * t + p, HALF:] = jnp.where(low, 0.0, qp).astype(BF16)

    def scores(g, j):
        p = g % 2
        keys = kc[j * BLK:(j + 1) * BLK, p * PAIR:(p + 1) * PAIR]
        s = lax.dot_general(qm[g], keys, NT, preferred_element_type=F32)
        sbuf[p, j] = s
        m = s[:, :PAIR]
        for i in range(1, BLK // PAIR):
            m = jnp.maximum(m, s[:, i * PAIR:(i + 1) * PAIR])
        mbuf[p] = m if j == 0 else jnp.maximum(mbuf[p], m)

    def weigh(g, j):
        p = g % 2
        top = mbuf[2 + p]
        e = [
            jnp.exp2(sbuf[p, j, :, i * PAIR:(i + 1) * PAIR] - top).astype(BF16)
            for i in range(BLK // PAIR)
        ]
        e = jnp.concatenate(e, axis=1)
        o = jnp.dot(e, vp[p, j * BLK:(j + 1) * BLK, :], preferred_element_type=F32)
        obuf[p] = o if j == 0 else obuf[p] + o

    def stage(g_weigh, g_score):
        for j in range(NB):
            if g_score is not None:
                scores(g_score, j)
            if g_weigh is not None:
                weigh(g_weigh, j)
        if g_score is not None:
            p = g_score % 2
            mbuf[2 + p] = jnp.broadcast_to(
                jnp.max(mbuf[p], axis=1, keepdims=True), (TOK, PAIR)
            )

    def finish(g):
        t, p = g // 2, g % 2
        o = obuf[p]
        o = o[:, :PAIR] / o[:, PAIR:]
        abuf[src, t * HALF:(t + 1) * HALF, p * PAIR:(p + 1) * PAIR] = jnp.where(
            low, o[:HALF], o[HALF:]
        ).astype(BF16)

    def o_part(owner, t):
        w = wo[pl.ds(pl.multiple_of(owner * FEAT, FEAT), FEAT), :]
        rows = slice(t * HALF, (t + 1) * HALF)
        qacc[rows, :] += jnp.dot(abuf[owner, rows, :], w, preferred_element_type=F32)

    stage(None, 0)
    stage(0, 1)
    finish(0)
    stage(1, 2)
    finish(1)
    att.own(0)
    stage(2, 3)
    finish(2)
    stage(3, None)
    finish(3)
    att.own(1)
    loads[4].wait()
    qacc[...] = jnp.zeros_like(qacc)
    o_part(src, 0)
    o_part(src, 1)
    for step in (
        (0, 1, 0), (0, 1, 1), 0, (0, 2, 0), 1, (0, 2, 1), (1, 1, 0), (0, 3, 0), (1, 1, 1),
        (0, 3, 1), (1, 2, 0), (0, 4, 0), (1, 2, 1), (0, 4, 1), (1, 3, 0), (1, 3, 1),
        (1, 4, 0), (1, 4, 1),
    ):
        if isinstance(step, int):
            att.cross(step)
            o_part(partner, step)
        else:
            for o in att.both(*step):
                o_part(o, step[2])

    out_ref[...] = qacc[...]
    for c in pending:
        c.wait_send()


def body(hidden_in, norm_gain, w_query, keys_cache, values_cache, lengths, w_output):
    gain = norm_gain.astype(F32).reshape(SRC, 1, FEAT)
    anywhere = pl.BlockSpec(memory_space=pl.ANY)
    vmem = pl.BlockSpec(memory_space=pltpu.VMEM)
    smem = pl.BlockSpec(memory_space=pltpu.SMEM)
    dma = pltpu.SemaphoreType.DMA
    branch = pl.pallas_call(
        kernel,
        out_shape=jax.ShapeDtypeStruct((TOK, FEAT), F32),
        in_specs=[anywhere, vmem, anywhere, anywhere, anywhere, smem, anywhere],
        out_specs=vmem,
        scratch_shapes=[
            pltpu.VMEM((SRC, TOK, FEAT), BF16),
            pltpu.VMEM((TGT, 2, POS, FEAT), BF16),
            pltpu.VMEM((WIDE, FEAT), BF16),
            pltpu.VMEM((2, WIDE, FEAT), BF16),
            pltpu.VMEM((WIDE, FEAT), BF16),
            pltpu.VMEM((WIDE, FEAT), BF16),
            pltpu.VMEM((SRC, TOK, FEAT), BF16),
            pltpu.VMEM((2, NB, TOK, BLK), F32),
            pltpu.VMEM((4, TOK, PAIR), F32),
            pltpu.VMEM((2, TOK, FEAT), F32),
            pltpu.VMEM((TOK, FEAT), F32),
            pltpu.VMEM((TOK, PAIR), F32),
            pltpu.VMEM((4, TOK, PAIR), BF16),
            pltpu.VMEM((8, FEAT), F32),
            dma((5,)),
            dma((32,)), dma((32,)),
            dma((32,)), dma((32,)),
            dma((80,)), dma((64,)),
        ],
        compiler_params=pltpu.CompilerParams(
            collective_id=0, has_side_effects=True, vmem_limit_bytes=63 * 1024 * 1024,
        ),
        cost_estimate=pl.CostEstimate(
            flops=6_000_000_000, bytes_accessed=8_000_000, transcendentals=4_200_000
        ),
    )(hidden_in, gain, w_query, keys_cache, values_cache, lengths, w_output)
    return hidden_in.astype(F32) + branch


def solution(mesh):
    in_specs = (
        P("tgt", "src"),
        P(),
        P(None, "src"),
        P("tgt", "src"),
        P("tgt", "src"),
        P(),
        P(None, "src"),
    )
    out_specs = P("tgt", "src")
    return jax.shard_map(body, mesh=mesh, in_specs=in_specs, out_specs=out_specs, check_vma=False)
```

time: 97.4 us -> 87.3 us (0.90)
  the two profiles are of different devices: /device:TPU:8 before, /device:TPU:4 now
where the time goes in v2:
time: 87.3 us; the launch traced here: 87.1 us
  Pallas kernels  84.1 us (96%)
  other arithmetic  2.98 us (3%)
    pallas_call x1, Pallas kernels, body(): pl.pallas_call(kernel, out_shape=jax.ShapeDtypeStruct((TOK, FEAT), F32),...  84.1 us

profile of v2, /device:TPU:4, one launch (start us, length us, event | category | flops | bytes accessed | tf_op | source)
XLA Modules:
  0.0 87.1 jit_solution(5179122821756586836)
XLA Ops:
  0.0 1.3 %reshape.7 = f32[4096]{0:T(1024)} convert(bf16[4096]{0:T(1024)(128)(2,1)} %param.8) | non-fusion elementwise | flops 4096 | bytes 24576 | tf_op jit(solution)/shard_map/reshape | solution.py:324
  1.3 0.0 copy-start
  1.3 84.1 %shard_map.73 = f32[256,256]{1,0:T(8,128)} custom-call(bf16[256,256]{1,0:T(8,128)(2,1)} %hid_hbm.1, f32[16,1,256]{2,1,0:T(1,128)} %bitcast.1, bf16[4096,256]{1,0:T(8,128)(2,1)} %wq_hbm.1, bf16[128,256]{1,0:T(8,128)(2,1)} %keys_hbm.1, bf16[128,256]{1,0:T(8,128)(2,1)} %vals_hbm.1, s32[16]{0:T(128)} %len_ref.1, bf16[4096,256]{1,0:T(8,128)(2,1)} %wo_hbm.1), custom_call_target="tpu_custom_call" | custom-call | flops 6000000000 | bytes 8000000 | tf_op jit(solution)/shard_map/pallas_call | solution.py:329
  85.4 0.0 copy-done
  85.4 1.7 %convert_add_fusion = f32[256,256]{1,0:T(8,128)} fusion(f32[256,256]{1,0:T(8,128)} %shard_map.73, bf16[256,256]{1,0:T(8,128)(2,1)S(1)} %copy-done), kind=kLoop, calls=%fused_computation | loop fusion | flops 131072 | bytes 655360 | tf_op jit(solution)/shard_map/add | solution.py:361
Async XLA Ops:
  1.3 84.1 %copy-start = (bf16[256,256]{1,0:T(8,128)(2,1)S(1)}, bf16[256,256]{1,0:T(8,128)(2,1)}, u32[]{:S(2)}) copy-start(bf16[256,256]{1,0:T(8,128)(2,1)} %hid_hbm.1) | copy-start | bytes 393220

commit v3 on v2

--- a/solution.py
+++ b/solution.py
@@ -14,6 +14,7 @@
 TOK, FEAT, POS, WIDE = 256, 256, 128, 4096
 PAIR = 128
 HALF = 128
+LAG = 6
 BLK = 512
 NB = WIDE // BLK
 SCALE = HD ** -0.5 * 1.4426950408889634
@@ -23,8 +24,8 @@
 
 def kernel(
     hid_hbm, gain_ref, wq_hbm, keys_hbm, vals_hbm, len_ref, wo_hbm, out_ref,
-    hbuf, kv, kc, vp, wq, wo, abuf, sbuf, mbuf, obuf, qacc, ssq, qm, krow,
-    loc_sem, h_send, h_recv, a_send, a_recv, kv_send, kv_recv,
+    hbuf, kv, kc, vp, wq, wo, wop, abuf, sbuf, mbuf, obuf, qacc, pacc, pbuf, rbuf, ssq, qm, krow,
+    loc_sem, h_send, h_recv, a_send, a_recv, kv_send, kv_recv, w_send, w_recv, p_send, p_recv,
 ):
     src = lax.axis_index("src")
     tgt = lax.axis_index("tgt")
@@ -106,18 +107,13 @@
                 self.push(owner, half, (z_right if way == "R" else z_left, tgt))
             return owner
 
-        def both(self, col, dist, half):
-            ways = "RL" if dist < 4 else ("R" if col == 0 else "L")
-            return [self.take(col, dist, way, half) for way in ways]
-
         def cross(self, half):
             arrived(self.slot(partner, half), self.rsem.at[partner * 2 + half])
             self.push(partner, half, (z_right, tgt))
             self.push(partner, half, (z_left, tgt))
 
     hid = Ring(lambda o, h: hbuf.at[o, pl.ds(h * HALF, HALF)], h_send, h_recv)
-    att = Ring(lambda o, h: abuf.at[o, pl.ds(h * HALF, HALF)], a_send, a_recv)
-    kv_count = [0]
+    kv_count, a_count, w_count = [0], [0], [0]
 
     def kv_push(s, u, dev):
         send(kv.at[s, u], kv_send.at[kv_count[0]], kv_recv.at[s * 2 + u], dev)
@@ -150,12 +146,15 @@
 
     for half in range(2):
         hid.own(half)
+    def own_y(u):
+        for k in (1, 3, 2):
+            kv_push(tgt, u, (src, at_tgt(x, yl + k)))
+
     for u in range(2):
         kv_push(tgt, u, (src, x_right))
         kv_push(tgt, u, (src, x_left))
-        for k in (1, 3, 2):
-            kv_push(tgt, u, (src, at_tgt(x, yl + k)))
         kv_push(tgt, u, (src, sib))
+    own_y(0)
 
     loads[3].wait()
     q_part(src)
@@ -174,16 +173,16 @@
         kv_push(s, u, (src, x_left))
         own_taken(s, u)
 
-    def take_x(k, u):
-        s_left, s_right = at_tgt(x + NX - 1, yl + k), at_tgt(x + 1, yl + k)
-        kv_wait(s_left, u)
-        if u == 0:
-            kv_push(s_left, u, (src, x_right))
-        kv_wait(s_right, u)
-        if u == 1:
-            kv_push(s_right, u, (src, x_left))
-        own_taken(s_left, u)
-        own_taken(s_right, u)
+    def take_x(k, u, way):
+        from_left = way == "l"
+        s = at_tgt(x + NX - 1 if from_left else x + 1, yl + k)
+        kv_wait(s, u)
+        far_right = (k in (0, 3)) == (u == 0)
+        if from_left and far_right:
+            kv_push(s, u, (src, x_right))
+        if not from_left and not far_right:
+            kv_push(s, u, (src, x_left))
+        own_taken(s, u)
 
     def take_far(k, u):
         s = at_tgt(x + 2, yl + k)
@@ -206,31 +205,91 @@
         prep(other, 0)
         backlog.append((other, 1))
 
-    def take_z(col, dist, half):
-        owners = hid.both(col, dist, half)
-        if half == 1:
-            for o in owners:
-                q_part(o)
-
-    def cross_z():
-        hid.cross(0)
-        hid.cross(1)
-
-    def cross_q():
-        q_part(partner)
-
-    Z, Y, X, W = take_z, take_y, take_x, take_far
+    halves = {}
+
+    def counted(key, owner):
+        halves[key] = halves.get(key, 0) + 1
+        if halves[key] == 2:
+            q_part(owner)
+
+    def take_z(col, dist, half, way):
+        counted((col, dist, way), hid.take(col, dist, way, half))
+
+    def cross_z(half):
+        hid.cross(half)
+        counted("cross", partner)
+
+    def wo_block(xx):
+        return (xx % NX) * 2 + core
+
+    def w_push(j, h, dev, ref=None):
+        dst = wop.at[j, pl.ds(h * HALF, HALF)]
+        c = pltpu.make_async_remote_copy(
+            src_ref=dst if ref is None else ref, dst_ref=dst,
+            send_sem=w_send.at[w_count[0]], recv_sem=w_recv.at[j * 2 + h],
+            device_id=dev, device_id_type=MESH,
+        )
+        c.start()
+        pending.append(c)
+        w_count[0] += 1
+
+    def w_wait(j, h):
+        arrived(wop.at[j, pl.ds(h * HALF, HALF)], w_recv.at[j * 2 + h])
+
+    def send_wo():
+        j = wo_block(x)
+        loads[4].wait()
+        for h in range(2):
+            row = pl.multiple_of((j * 2 + 1 - yh) * FEAT + h * HALF, HALF)
+            w_push(j, h, (partner, tgt), wo.at[pl.ds(row, HALF)])
+
+    def share_wo():
+        j = wo_block(x)
+        for h in range(2):
+            w_wait(j, h)
+            w_push(j, h, (src, x_right))
+            w_push(j, h, (src, x_left))
+            w_push(j, h, (src, sib))
+
+    def share_wo_x():
+        j_left, j_right = wo_block(x + NX - 1), wo_block(x + 1)
+        w_wait(j_left, 0)
+        w_push(j_left, 0, (src, x_right))
+        w_wait(j_right, 1)
+        w_push(j_right, 1, (src, x_left))
+        w_wait(j_left, 1)
+        w_wait(j_right, 0)
+        for h in range(2):
+            w_push(j_left, h, (src, sib))
+            w_push(j_right, h, (src, sib))
+
+    def share_wo_far():
+        j = wo_block(x + 2)
+        for h in range(2):
+            w_wait(j, h)
+            w_push(j, h, (src, sib))
+
+    def share_wo_end():
+        for xx in range(NX):
+            for h in range(2):
+                w_wait(xx * 2 + 1 - core, h)
+
+    Z, C, F, Y, X, W, O = take_z, cross_z, first_row, take_y, take_x, take_far, send_wo
+    V = functools.partial(own_y, 1)
     for event in (
-        (Z, 0, 1, 0), (first_row,), (X, 0, 0), (Z, 0, 1, 1), (Y, 1, 0), (X, 0, 1),
-        (Y, 3, 0), (cross_z,), (Z, 0, 2, 0), (W, 0, 0), (cross_q,), (Z, 1, 1, 0), (Y, 2, 0),
-        (X, 1, 0), (Z, 0, 2, 1), (W, 0, 1), (Y, 1, 1), (Z, 1, 1, 1), (X, 3, 0),
-        (W, 1, 0), (Z, 0, 3, 0), (Y, 3, 1), (X, 2, 0), (Z, 1, 2, 0), (W, 3, 0),
-        (Z, 0, 3, 1), (X, 1, 1), (Y, 2, 1), (Z, 1, 2, 1), (W, 2, 0), (Z, 0, 4, 0),
-        (W, 1, 1), (X, 3, 1), (Z, 1, 3, 0), (Z, 0, 4, 1), (X, 2, 1), (W, 3, 1),
-        (Z, 1, 3, 1), (Z, 1, 4, 0), (W, 2, 1), (Z, 1, 4, 1),
+        (Z, 0, 1, 0, "R"), (F,), (X, 0, 0, "r"), (Z, 0, 1, 0, "L"), (V,), (X, 0, 0, "l"), (Z, 0, 1, 1, "R"),
+        (X, 0, 1, "l"), (Z, 0, 1, 1, "L"), (Z, 0, 2, 0, "R"), (X, 0, 1, "r"), (Z, 0, 2, 0, "L"),
+        (Z, 0, 2, 1, "R"), (W, 0, 0), (Z, 0, 2, 1, "L"), (Y, 3, 0), (C, 0), (Y, 1, 0), (W, 0, 1), (Y, 2, 0),
+        (C, 1), (Z, 0, 3, 0, "R"), (Z, 0, 3, 1, "R"), (Z, 0, 3, 1, "L"), (X, 3, 0, "l"), (X, 3, 0, "r"),
+        (Z, 1, 1, 0, "L"), (Z, 0, 3, 0, "L"), (X, 1, 0, "r"), (Z, 1, 1, 1, "R"), (Z, 1, 1, 0, "R"),
+        (Z, 1, 1, 1, "L"), (Y, 1, 1), (Y, 3, 1), (Y, 2, 1), (Z, 1, 2, 0, "L"), (W, 3, 0), (O,), (X, 2, 0, "l"),
+        (Z, 0, 4, 1, "R"), (X, 2, 0, "r"), (Z, 1, 2, 1, "L"), (W, 1, 0), (X, 1, 0, "l"), (Z, 1, 2, 1, "R"),
+        (X, 1, 1, "l"), (Z, 0, 4, 0, "R"), (X, 1, 1, "r"), (Z, 1, 3, 0, "L"), (X, 3, 1, "r"), (Z, 1, 2, 0, "R"),
+        (X, 2, 1, "l"), (Z, 1, 3, 1, "L"), (X, 3, 1, "l"), (Z, 1, 3, 1, "R"), (W, 1, 1), (W, 2, 0),
+        (X, 2, 1, "r"), (Z, 1, 4, 0, "L"), (Z, 1, 3, 0, "R"), (W, 2, 1), (W, 3, 1), (Z, 1, 4, 1, "L"),
     ):
         event[0](*event[1:])
-        drain(4)
+        drain(LAG)
     drain(0)
 
     mean = jnp.sum(ssq[...], axis=1, keepdims=True) / WIDE
@@ -279,43 +338,74 @@
         t, p = g // 2, g % 2
         o = obuf[p]
         o = o[:, :PAIR] / o[:, PAIR:]
-        abuf[src, t * HALF:(t + 1) * HALF, p * PAIR:(p + 1) * PAIR] = jnp.where(
+        abuf[z, t * HALF:(t + 1) * HALF, p * PAIR:(p + 1) * PAIR] = jnp.where(
             low, o[:HALF], o[HALF:]
         ).astype(BF16)
 
-    def o_part(owner, t):
-        w = wo[pl.ds(pl.multiple_of(owner * FEAT, FEAT), FEAT), :]
+    def a_push(zz, t, dev):
+        ref = abuf.at[zz, pl.ds(t * HALF, HALF)]
+        send(ref, a_send.at[a_count[0]], a_recv.at[zz * 2 + t], dev)
+        a_count[0] += 1
+
+    def a_own(t):
+        a_push(z, t, (z_right, tgt))
+        a_push(z, t, (z_left, tgt))
+
+    def o_part(zz, t):
         rows = slice(t * HALF, (t + 1) * HALF)
-        qacc[rows, :] += jnp.dot(abuf[owner, rows, :], w, preferred_element_type=F32)
+        a = abuf[zz, rows, :]
+        w = wo[pl.ds(pl.multiple_of((zz * 2 + yh) * FEAT, FEAT), FEAT), :]
+        qacc[rows, :] += jnp.dot(a, w, preferred_element_type=F32)
+        pacc[rows, :] += jnp.dot(a, wop[zz], preferred_element_type=F32)
+
+    def a_take(dist, t):
+        taken = []
+        for way in "RL" if dist < 4 else "RL"[t]:
+            zz = (z - dist + NZ) % NZ if way == "R" else (z + dist) % NZ
+            arrived(abuf.at[zz, pl.ds(t * HALF, HALF)], a_recv.at[zz * 2 + t])
+            if dist < 3 or (dist == 3 and way == "RL"[t]):
+                a_push(zz, t, (z_right if way == "R" else z_left, tgt))
+            taken.append(zz)
+        for zz in taken:
+            o_part(zz, t)
+
+    def exchange(t):
+        pbuf[t] = pacc[t * HALF:(t + 1) * HALF, :].astype(BF16)
+        c = pltpu.make_async_remote_copy(
+            src_ref=pbuf.at[t], dst_ref=rbuf.at[t], send_sem=p_send.at[t], recv_sem=p_recv.at[t],
+            device_id=(partner, tgt), device_id_type=MESH,
+        )
+        c.start()
+        pending.append(c)
 
     stage(None, 0)
+    share_wo()
     stage(0, 1)
     finish(0)
     stage(1, 2)
     finish(1)
-    att.own(0)
+    a_own(0)
+    share_wo_x()
     stage(2, 3)
     finish(2)
     stage(3, None)
     finish(3)
-    att.own(1)
-    loads[4].wait()
+    a_own(1)
+    share_wo_far()
     qacc[...] = jnp.zeros_like(qacc)
-    o_part(src, 0)
-    o_part(src, 1)
-    for step in (
-        (0, 1, 0), (0, 1, 1), 0, (0, 2, 0), 1, (0, 2, 1), (1, 1, 0), (0, 3, 0), (1, 1, 1),
-        (0, 3, 1), (1, 2, 0), (0, 4, 0), (1, 2, 1), (0, 4, 1), (1, 3, 0), (1, 3, 1),
-        (1, 4, 0), (1, 4, 1),
-    ):
-        if isinstance(step, int):
-            att.cross(step)
-            o_part(partner, step)
-        else:
-            for o in att.both(*step):
-                o_part(o, step[2])
-
-    out_ref[...] = qacc[...]
+    pacc[...] = jnp.zeros_like(pacc)
+    share_wo_end()
+    o_part(z, 0)
+    o_part(z, 1)
+    for dist, t in ((1, 0), (1, 1), (2, 0), (2, 1), (3, 0), (3, 1), (4, 0)):
+        a_take(dist, t)
+    exchange(0)
+    a_take(4, 1)
+    exchange(1)
+    for t in range(2):
+        arrived(rbuf.at[t], p_recv.at[t])
+        rows = slice(t * HALF, (t + 1) * HALF)
+        out_ref[rows, :] = qacc[rows, :] + rbuf[t].astype(F32)
     for c in pending:
         c.wait_send()
 
@@ -338,18 +428,22 @@
             pltpu.VMEM((2, WIDE, FEAT), BF16),
             pltpu.VMEM((WIDE, FEAT), BF16),
             pltpu.VMEM((WIDE, FEAT), BF16),
-            pltpu.VMEM((SRC, TOK, FEAT), BF16),
+            pltpu.VMEM((NZ, FEAT, FEAT), BF16),
+            pltpu.VMEM((NZ, TOK, FEAT), BF16),
             pltpu.VMEM((2, NB, TOK, BLK), F32),
             pltpu.VMEM((4, TOK, PAIR), F32),
             pltpu.VMEM((2, TOK, FEAT), F32),
             pltpu.VMEM((TOK, FEAT), F32),
+            pltpu.VMEM((TOK, FEAT), F32),
+            pltpu.VMEM((2, HALF, FEAT), BF16),
+            pltpu.VMEM((2, HALF, FEAT), BF16),
             pltpu.VMEM((TOK, PAIR), F32),
             pltpu.VMEM((4, TOK, PAIR), BF16),
             pltpu.VMEM((8, FEAT), F32),
             dma((5,)),
             dma((32,)), dma((32,)),
-            dma((32,)), dma((32,)),
-            dma((80,)), dma((64,)),
+            dma((16,)), dma((16,)),
+            dma((80,)), dma((64,)), dma((20,)), dma((16,)), dma((2,)), dma((2,)),
         ],
         compiler_params=pltpu.CompilerParams(
             collective_id=0, has_side_effects=True, vmem_limit_bytes=63 * 1024 * 1024,

time: 87.3 us -> 82.5 us (0.945)
  the two profiles are of different devices: /device:TPU:4 before, /device:TPU:1 now
where the time goes in v3:
time: 82.5 us; the launch traced here: 82.3 us
  Pallas kernels  79.3 us (96%)
  other arithmetic  2.98 us (4%)
    pallas_call x1, Pallas kernels, body(): pl.pallas_call(kernel, out_shape=jax.ShapeDtypeStruct((TOK, FEAT), F32),...  79.3 us
    add x1, other arithmetic, body(): return hidden_in.astype(F32) + branch  1.68 us

profile of v3, /device:TPU:1, one launch (start us, length us, event | category | flops | bytes accessed | tf_op | source)
XLA Modules:
  0.0 82.3 jit_solution(10229047553712354031)
XLA Ops:
  0.0 1.3 %reshape.7 = f32[4096]{0:T(1024)} convert(bf16[4096]{0:T(1024)(128)(2,1)} %param.8) | non-fusion elementwise | flops 4096 | bytes 24576 | tf_op jit(solution)/shard_map/reshape | solution.py:414
  1.3 0.0 copy-start
  1.3 79.3 %shard_map.73 = f32[256,256]{1,0:T(8,128)} custom-call(bf16[256,256]{1,0:T(8,128)(2,1)} %hid_hbm.1, f32[16,1,256]{2,1,0:T(1,128)} %bitcast.1, bf16[4096,256]{1,0:T(8,128)(2,1)} %wq_hbm.1, bf16[128,256]{1,0:T(8,128)(2,1)} %keys_hbm.1, bf16[128,256]{1,0:T(8,128)(2,1)} %vals_hbm.1, s32[16]{0:T(128)} %len_ref.1, bf16[4096,256]{1,0:T(8,128)(2,1)} %wo_hbm.1), custom_call_target="tpu_custom_call" | custom-call | flops 6000000000 | bytes 8000000 | tf_op jit(solution)/shard_map/pallas_call | solution.py:419
  80.6 0.0 copy-done
  80.6 1.7 %convert_add_fusion = f32[256,256]{1,0:T(8,128)} fusion(f32[256,256]{1,0:T(8,128)} %shard_map.73, bf16[256,256]{1,0:T(8,128)(2,1)S(1)} %copy-done), kind=kLoop, calls=%fused_computation | loop fusion | flops 131072 | bytes 655360 | tf_op jit(solution)/shard_map/add | solution.py:455
Async XLA Ops:
  1.3 79.3 %copy-start = (bf16[256,256]{1,0:T(8,128)(2,1)S(1)}, bf16[256,256]{1,0:T(8,128)(2,1)}, u32[]{:S(2)}) copy-start(bf16[256,256]{1,0:T(8,128)(2,1)} %hid_hbm.1) | copy-start | bytes 393220

commit v4 on v3

--- a/solution.py
+++ b/solution.py
@@ -40,6 +40,13 @@
         return (xx % NX) * 8 + (yy % NYL) * 2 + core
 
     x_right, x_left = at_tgt(x + 1, yl), at_tgt(x + NX - 1, yl)
+    edge = yl == 0
+    rows_from = [
+        yl,
+        jnp.where(edge, 1, yl - 1),
+        jnp.where(edge, 2, jnp.where(yl == 3, 1, yl + 1)),
+        jnp.where(yl < 2, 3, 0),
+    ]
 
     loads = [
         pltpu.make_async_copy(hid_hbm, hbuf.at[src], loc_sem.at[0]),
@@ -55,7 +62,7 @@
     friends = [
         (partner, tgt), (z_right, tgt), (z_left, tgt),
         (src, x_right), (src, x_left), (src, sib),
-        (src, at_tgt(x, yl + 1)), (src, at_tgt(x, yl + 2)), (src, at_tgt(x, yl + 3)),
+        (src, at_tgt(x, yl + 1)), (src, at_tgt(x, yl + NYL - 1)),
     ]
     for f in friends:
         pl.semaphore_signal(barrier, inc=1, device_id=f, device_id_type=MESH)
@@ -66,7 +73,7 @@
         c.wait()
     pl.semaphore_wait(barrier, len(friends))
 
-    pending = []
+    pending, guarded = [], []
 
     def send(ref, ssem, rsem, dev):
         c = pltpu.make_async_remote_copy(
@@ -146,15 +153,26 @@
 
     for half in range(2):
         hid.own(half)
-    def own_y(u):
-        for k in (1, 3, 2):
-            kv_push(tgt, u, (src, at_tgt(x, yl + k)))
+    def at_yl(yy):
+        return x * 8 + yy * 2 + core
+
+    def maybe(when, s, u, dev):
+        i = kv_count[0]
+        kv_count[0] += 1
+        c = pltpu.make_async_remote_copy(
+            src_ref=kv.at[s, u], dst_ref=kv.at[s, u], send_sem=kv_send.at[i],
+            recv_sem=kv_recv.at[s * 2 + u], device_id=dev, device_id_type=MESH,
+        )
+        pl.when(when)(c.start)
+        guarded.append((when, c))
 
     for u in range(2):
+        maybe(yl < NYL - 1, tgt, u, (src, at_yl(jnp.minimum(yl + 1, NYL - 1))))
+        maybe(yl > 0, tgt, u, (src, at_yl(jnp.maximum(yl - 1, 0))))
         kv_push(tgt, u, (src, x_right))
         kv_push(tgt, u, (src, x_left))
         kv_push(tgt, u, (src, sib))
-    own_y(0)
+    inner = (yl > 0) & (yl < NYL - 1)
 
     loads[3].wait()
     q_part(src)
@@ -167,15 +185,17 @@
         backlog.append((s + 1 - 2 * core, u))
 
     def take_y(k, u):
-        s = at_tgt(x, yl + k)
+        s = at_yl(rows_from[k])
         kv_wait(s, u)
+        onward = jnp.where(rows_from[k] > yl, yl - 1, yl + 1)
+        maybe(inner, s, u, (src, at_yl(jnp.clip(onward, 0, NYL - 1))))
         kv_push(s, u, (src, x_right))
         kv_push(s, u, (src, x_left))
         own_taken(s, u)
 
     def take_x(k, u, way):
         from_left = way == "l"
-        s = at_tgt(x + NX - 1 if from_left else x + 1, yl + k)
+        s = at_tgt(x + NX - 1 if from_left else x + 1, rows_from[k])
         kv_wait(s, u)
         far_right = (k in (0, 3)) == (u == 0)
         if from_left and far_right:
@@ -185,15 +205,20 @@
         own_taken(s, u)
 
     def take_far(k, u):
-        s = at_tgt(x + 2, yl + k)
+        s = at_tgt(x + 2, rows_from[k])
         kv_wait(s, u)
         own_taken(s, u)
 
-    def drain(keep):
-        while len(backlog) > keep:
-            s, u = backlog.pop(0)
-            kv_wait(s, u)
-            prep(s, u)
+    def drain(keep, only=None):
+        spare = len(backlog) - keep if only is None else len(backlog)
+        kept = []
+        for i, (s, u) in enumerate(backlog):
+            if i < spare and only in (None, u):
+                kv_wait(s, u)
+                prep(s, u)
+            else:
+                kept.append((s, u))
+        backlog[:] = kept
 
     def first_row():
         other = tgt + 1 - 2 * core
@@ -243,63 +268,52 @@
             row = pl.multiple_of((j * 2 + 1 - yh) * FEAT + h * HALF, HALF)
             w_push(j, h, (partner, tgt), wo.at[pl.ds(row, HALF)])
 
-    def share_wo():
+    def take_wo(h):
         j = wo_block(x)
-        for h in range(2):
-            w_wait(j, h)
+        w_wait(j, h)
+        w_push(j, h, (src, x_right))
+        w_push(j, h, (src, x_left))
+        w_push(j, h, (src, sib))
+
+    def take_wo_x(h, way):
+        j = wo_block(x + NX - 1 if way == "l" else x + 1)
+        w_wait(j, h)
+        if (h, way) == (0, "l"):
             w_push(j, h, (src, x_right))
+        if (h, way) == (1, "r"):
             w_push(j, h, (src, x_left))
-            w_push(j, h, (src, sib))
-
-    def share_wo_x():
-        j_left, j_right = wo_block(x + NX - 1), wo_block(x + 1)
-        w_wait(j_left, 0)
-        w_push(j_left, 0, (src, x_right))
-        w_wait(j_right, 1)
-        w_push(j_right, 1, (src, x_left))
-        w_wait(j_left, 1)
-        w_wait(j_right, 0)
-        for h in range(2):
-            w_push(j_left, h, (src, sib))
-            w_push(j_right, h, (src, sib))
-
-    def share_wo_far():
+        w_push(j, h, (src, sib))
+
+    def take_wo_far(h):
         j = wo_block(x + 2)
-        for h in range(2):
-            w_wait(j, h)
-            w_push(j, h, (src, sib))
-
-    def share_wo_end():
+        w_wait(j, h)
+        w_push(j, h, (src, sib))
+
+    ready, todo = [], []
+
+    def flush():
+        while ready and todo:
+            o_part(*todo.pop(0))
+
+    def end_wo():
         for xx in range(NX):
             for h in range(2):
                 w_wait(xx * 2 + 1 - core, h)
-
-    Z, C, F, Y, X, W, O = take_z, cross_z, first_row, take_y, take_x, take_far, send_wo
-    V = functools.partial(own_y, 1)
-    for event in (
-        (Z, 0, 1, 0, "R"), (F,), (X, 0, 0, "r"), (Z, 0, 1, 0, "L"), (V,), (X, 0, 0, "l"), (Z, 0, 1, 1, "R"),
-        (X, 0, 1, "l"), (Z, 0, 1, 1, "L"), (Z, 0, 2, 0, "R"), (X, 0, 1, "r"), (Z, 0, 2, 0, "L"),
-        (Z, 0, 2, 1, "R"), (W, 0, 0), (Z, 0, 2, 1, "L"), (Y, 3, 0), (C, 0), (Y, 1, 0), (W, 0, 1), (Y, 2, 0),
-        (C, 1), (Z, 0, 3, 0, "R"), (Z, 0, 3, 1, "R"), (Z, 0, 3, 1, "L"), (X, 3, 0, "l"), (X, 3, 0, "r"),
-        (Z, 1, 1, 0, "L"), (Z, 0, 3, 0, "L"), (X, 1, 0, "r"), (Z, 1, 1, 1, "R"), (Z, 1, 1, 0, "R"),
-        (Z, 1, 1, 1, "L"), (Y, 1, 1), (Y, 3, 1), (Y, 2, 1), (Z, 1, 2, 0, "L"), (W, 3, 0), (O,), (X, 2, 0, "l"),
-        (Z, 0, 4, 1, "R"), (X, 2, 0, "r"), (Z, 1, 2, 1, "L"), (W, 1, 0), (X, 1, 0, "l"), (Z, 1, 2, 1, "R"),
-        (X, 1, 1, "l"), (Z, 0, 4, 0, "R"), (X, 1, 1, "r"), (Z, 1, 3, 0, "L"), (X, 3, 1, "r"), (Z, 1, 2, 0, "R"),
-        (X, 2, 1, "l"), (Z, 1, 3, 1, "L"), (X, 3, 1, "l"), (Z, 1, 3, 1, "R"), (W, 1, 1), (W, 2, 0),
-        (X, 2, 1, "r"), (Z, 1, 4, 0, "L"), (Z, 1, 3, 0, "R"), (W, 2, 1), (W, 3, 1), (Z, 1, 4, 1, "L"),
-    ):
-        event[0](*event[1:])
-        drain(LAG)
-    drain(0)
-
-    mean = jnp.sum(ssq[...], axis=1, keepdims=True) / WIDE
-    q = qacc[...] * (lax.rsqrt(mean + 1e-06) * SCALE)
+        ready.append(1)
+        flush()
+
     low = lax.broadcasted_iota(jnp.int32, (HALF, PAIR), 1) < HD
-    for t in range(2):
-        for p in range(2):
-            qp = q[t * HALF:(t + 1) * HALF, p * PAIR:(p + 1) * PAIR]
-            qm[2 * t + p, :HALF] = jnp.where(low, qp, 0.0).astype(BF16)
-            qm[2 * t + p, HALF:] = jnp.where(low, 0.0, qp).astype(BF16)
+
+    def make_queries():
+        mean = jnp.sum(ssq[...], axis=1, keepdims=True) / WIDE
+        q = qacc[...] * (lax.rsqrt(mean + 1e-06) * SCALE)
+        for t in range(2):
+            for p in range(2):
+                qp = q[t * HALF:(t + 1) * HALF, p * PAIR:(p + 1) * PAIR]
+                qm[2 * t + p, :HALF] = jnp.where(low, qp, 0.0).astype(BF16)
+                qm[2 * t + p, HALF:] = jnp.where(low, 0.0, qp).astype(BF16)
+        qacc[...] = jnp.zeros_like(qacc)
+        pacc[...] = jnp.zeros_like(pacc)
 
     def scores(g, j):
         p = g % 2
@@ -358,16 +372,13 @@
         qacc[rows, :] += jnp.dot(a, w, preferred_element_type=F32)
         pacc[rows, :] += jnp.dot(a, wop[zz], preferred_element_type=F32)
 
-    def a_take(dist, t):
-        taken = []
-        for way in "RL" if dist < 4 else "RL"[t]:
-            zz = (z - dist + NZ) % NZ if way == "R" else (z + dist) % NZ
-            arrived(abuf.at[zz, pl.ds(t * HALF, HALF)], a_recv.at[zz * 2 + t])
-            if dist < 3 or (dist == 3 and way == "RL"[t]):
-                a_push(zz, t, (z_right if way == "R" else z_left, tgt))
-            taken.append(zz)
-        for zz in taken:
-            o_part(zz, t)
+    def a_take(dist, t, way):
+        zz = (z - dist + NZ) % NZ if way == "R" else (z + dist) % NZ
+        arrived(abuf.at[zz, pl.ds(t * HALF, HALF)], a_recv.at[zz * 2 + t])
+        if dist < 3 or (dist == 3 and way == "RL"[t]):
+            a_push(zz, t, (z_right if way == "R" else z_left, tgt))
+        todo.append((zz, t))
+        flush()
 
     def exchange(t):
         pbuf[t] = pacc[t * HALF:(t + 1) * HALF, :].astype(BF16)
@@ -378,36 +389,52 @@
         c.start()
         pending.append(c)
 
-    stage(None, 0)
-    share_wo()
-    stage(0, 1)
-    finish(0)
-    stage(1, 2)
-    finish(1)
-    a_own(0)
-    share_wo_x()
-    stage(2, 3)
-    finish(2)
-    stage(3, None)
-    finish(3)
-    a_own(1)
-    share_wo_far()
-    qacc[...] = jnp.zeros_like(qacc)
-    pacc[...] = jnp.zeros_like(pacc)
-    share_wo_end()
-    o_part(z, 0)
-    o_part(z, 1)
-    for dist, t in ((1, 0), (1, 1), (2, 0), (2, 1), (3, 0), (3, 1), (4, 0)):
-        a_take(dist, t)
-    exchange(0)
-    a_take(4, 1)
-    exchange(1)
+    def attend(n):
+        if n == 0:
+            drain(0, 0)
+            make_queries()
+        if n == 1:
+            drain(0)
+        stage(n - 1 if n else None, n if n < 4 else None)
+        if n:
+            finish(n - 1)
+        if n in (2, 4):
+            t = n // 2 - 1
+            a_own(t)
+            todo.append((z, t))
+            flush()
+
+    Z, C, F, Y, X, W = take_z, cross_z, first_row, take_y, take_x, take_far
+    O, OY, OX, OF, OE = send_wo, take_wo, take_wo_x, take_wo_far, end_wo
+    S, A, E = attend, a_take, exchange
+    for event in (
+        (Z, 0, 1, 0, "R"), (Z, 0, 1, 0, "L"), (F,), (Y, 1, 0), (X, 0, 0, "r"), (X, 0, 0, "l"),
+        (Z, 0, 1, 1, "R"), (X, 0, 1, "l"), (X, 0, 1, "r"), (Z, 0, 1, 1, "L"), (Y, 1, 1), (Z, 0, 2, 0, "R"),
+        (Z, 0, 2, 0, "L"), (X, 1, 0, "l"), (X, 1, 0, "r"), (Y, 2, 0), (C, 0), (W, 0, 0), (Z, 0, 2, 1, "R"),
+        (C, 1), (Z, 0, 2, 1, "L"), (Y, 2, 1), (X, 1, 1, "l"), (Y, 3, 0), (Z, 0, 3, 0, "R"), (X, 2, 0, "l"),
+        (Z, 1, 1, 0, "L"), (X, 1, 1, "r"), (Z, 1, 1, 0, "R"), (W, 0, 1), (X, 2, 0, "r"), (Z, 1, 1, 1, "L"),
+        (X, 2, 1, "l"), (Y, 3, 1), (O,), (Z, 1, 1, 1, "R"), (W, 1, 0), (Z, 1, 2, 0, "L"),
+        (Z, 0, 3, 1, "R"), (X, 3, 0, "l"), (W, 1, 1), (Z, 1, 2, 0, "R"), (Z, 1, 2, 1, "L"), (W, 2, 1),
+        (X, 2, 1, "r"), (Z, 0, 3, 1, "L"), (X, 3, 1, "r"), (Z, 1, 3, 0, "L"), (W, 2, 0), (Z, 1, 2, 1, "R"),
+        (X, 3, 1, "l"), (X, 3, 0, "r"), (Z, 1, 3, 1, "L"), (W, 3, 0), (Z, 0, 3, 0, "L"), (Z, 0, 4, 1, "R"),
+        (OY, 0), (Z, 0, 4, 0, "R"), (W, 3, 1), (Z, 1, 4, 0, "L"), (Z, 1, 3, 0, "R"), (Z, 1, 3, 1, "R"),
+        (OY, 1), (Z, 1, 4, 1, "L"), (S, 0), (S, 1), (OX, 0, "l"), (S, 2), (OX, 1, "r"), (S, 3), (S, 4),
+        (OX, 1, "l"), (OX, 0, "r"), (OF, 1), (OF, 0), (A, 1, 0, "R"), (A, 1, 0, "L"), (OE,),
+        (A, 1, 1, "L"), (A, 2, 0, "R"), (A, 2, 0, "L"), (A, 1, 1, "R"), (A, 2, 1, "L"), (A, 3, 0, "R"),
+        (A, 3, 0, "L"), (A, 2, 1, "R"), (A, 3, 1, "L"), (A, 4, 0, "R"), (E, 0), (A, 3, 1, "R"),
+        (A, 4, 1, "L"), (E, 1),
+    ):
+        event[0](*event[1:])
+        drain(LAG)
+
     for t in range(2):
         arrived(rbuf.at[t], p_recv.at[t])
         rows = slice(t * HALF, (t + 1) * HALF)
         out_ref[rows, :] = qacc[rows, :] + rbuf[t].astype(F32)
     for c in pending:
         c.wait_send()
+    for when, c in guarded:
+        pl.when(when)(c.wait_send)
 
 
 def body(hidden_in, norm_gain, w_query, keys_cache, values_cache, lengths, w_output):
@@ -443,7 +470,7 @@
             dma((5,)),
             dma((32,)), dma((32,)),
             dma((16,)), dma((16,)),
-            dma((80,)), dma((64,)), dma((20,)), dma((16,)), dma((2,)), dma((2,)),
+            dma((100,)), dma((64,)), dma((20,)), dma((16,)), dma((2,)), dma((2,)),
         ],
         compiler_params=pltpu.CompilerParams(
             collective_id=0, has_side_effects=True, vmem_limit_bytes=63 * 1024 * 1024,

time: 82.5 us -> 80 us (0.970)
  the two profiles are of different devices: /device:TPU:1 before, /device:TPU:2 now
where the time goes in v4:
time: 80 us; the launch traced here: 79.7 us
  Pallas kernels  76.7 us (96%)
  other arithmetic  2.98 us (4%)
    pallas_call x1, Pallas kernels, body(): pl.pallas_call(kernel, out_shape=jax.ShapeDtypeStruct((TOK, FEAT), F32),...  76.7 us
    add x1, other arithmetic, body(): return hidden_in.astype(F32) + branch  1.68 us

profile of v4, /device:TPU:2, one launch (start us, length us, event | category | flops | bytes accessed | tf_op | source)
XLA Modules:
  0.0 79.7 jit_solution(11791195145738663974)
XLA Ops:
  0.0 1.3 %reshape.7 = f32[4096]{0:T(1024)} convert(bf16[4096]{0:T(1024)(128)(2,1)} %param.8) | non-fusion elementwise | flops 4096 | bytes 24576 | tf_op jit(solution)/shard_map/reshape | solution.py:441
  1.3 0.0 copy-start
  1.3 76.7 %shard_map.73 = f32[256,256]{1,0:T(8,128)} custom-call(bf16[256,256]{1,0:T(8,128)(2,1)} %hid_hbm.1, f32[16,1,256]{2,1,0:T(1,128)} %bitcast.1, bf16[4096,256]{1,0:T(8,128)(2,1)} %wq_hbm.1, bf16[128,256]{1,0:T(8,128)(2,1)} %keys_hbm.1, bf16[128,256]{1,0:T(8,128)(2,1)} %vals_hbm.1, s32[16]{0:T(128)} %len_ref.1, bf16[4096,256]{1,0:T(8,128)(2,1)} %wo_hbm.1), custom_call_target="tpu_custom_call" | custom-call | flops 6000000000 | bytes 8000000 | tf_op jit(solution)/shard_map/pallas_call | solution.py:446
  78.0 0.0 copy-done
  78.0 1.7 %convert_add_fusion = f32[256,256]{1,0:T(8,128)} fusion(f32[256,256]{1,0:T(8,128)} %shard_map.73, bf16[256,256]{1,0:T(8,128)(2,1)S(1)} %copy-done), kind=kLoop, calls=%fused_computation | loop fusion | flops 131072 | bytes 655360 | tf_op jit(solution)/shard_map/add | solution.py:482
Async XLA Ops:
  1.3 76.7 %copy-start = (bf16[256,256]{1,0:T(8,128)(2,1)S(1)}, bf16[256,256]{1,0:T(8,128)(2,1)}, u32[]{:S(2)}) copy-start(bf16[256,256]{1,0:T(8,128)(2,1)} %hid_hbm.1) | copy-start | bytes 393220

commit v5 on v4

--- a/solution.py
+++ b/solution.py
@@ -23,8 +23,8 @@
 
 
 def kernel(
-    hid_hbm, gain_ref, wq_hbm, keys_hbm, vals_hbm, len_ref, wo_hbm, out_ref,
-    hbuf, kv, kc, vp, wq, wo, wop, abuf, sbuf, mbuf, obuf, qacc, pacc, pbuf, rbuf, ssq, qm, krow,
+    hid_hbm, gain_in, wq_hbm, keys_hbm, vals_hbm, len_ref, wo_hbm, out_ref,
+    hbuf, kv, kc, vp, wq, wo, wop, abuf, sbuf, mbuf, obuf, qacc, pacc, pbuf, rbuf, ssq, qm, krow, gain_ref,
     loc_sem, h_send, h_recv, a_send, a_recv, kv_send, kv_recv, w_send, w_recv, p_send, p_recv,
 ):
     src = lax.axis_index("src")
@@ -67,6 +67,8 @@
     for f in friends:
         pl.semaphore_signal(barrier, inc=1, device_id=f, device_id_type=MESH)
 
+    for o in range(SRC):
+        gain_ref[o] = gain_in[o * FEAT:(o + 1) * FEAT].astype(F32).reshape(1, FEAT)
     qacc[...] = jnp.zeros_like(qacc)
     ssq[...] = jnp.zeros_like(ssq)
     for c in loads[:3]:
@@ -438,7 +440,6 @@
 
 
 def body(hidden_in, norm_gain, w_query, keys_cache, values_cache, lengths, w_output):
-    gain = norm_gain.astype(F32).reshape(SRC, 1, FEAT)
     anywhere = pl.BlockSpec(memory_space=pl.ANY)
     vmem = pl.BlockSpec(memory_space=pltpu.VMEM)
     smem = pl.BlockSpec(memory_space=pltpu.SMEM)
@@ -467,6 +468,7 @@
             pltpu.VMEM((TOK, PAIR), F32),
             pltpu.VMEM((4, TOK, PAIR), BF16),
             pltpu.VMEM((8, FEAT), F32),
+            pltpu.VMEM((SRC, 1, FEAT), F32),
             dma((5,)),
             dma((32,)), dma((32,)),
             dma((16,)), dma((16,)),
@@ -478,7 +480,7 @@
         cost_estimate=pl.CostEstimate(
             flops=6_000_000_000, bytes_accessed=8_000_000, transcendentals=4_200_000
         ),
-    )(hidden_in, gain, w_query, keys_cache, values_cache, lengths, w_output)
+    )(hidden_in, norm_gain, w_query, keys_cache, values_cache, lengths, w_output)
     return hidden_in.astype(F32) + branch
 
 

time: 80 us -> 78.6 us (0.982)
  other arithmetic: 2.98 us -> 1.68 us
    reshape x1 -> x0, other arithmetic: 1.3 us -> none  [body(): gain = norm_gain.astype(F32).reshape(SRC, 1, FEAT)]
where the time goes in v5:
time: 78.6 us; the launch traced here: 78.4 us
  Pallas kernels  76.7 us (98%)
  other arithmetic  1.68 us (2%)
    pallas_call x1, Pallas kernels, body(): pl.pallas_call(kernel, out_shape=jax.ShapeDtypeStruct((TOK, FEAT), F32),...  76.7 us
    add x1, other arithmetic, body(): return hidden_in.astype(F32) + branch  1.68 us

profile of v5, /device:TPU:2, one launch (start us, length us, event | category | flops | bytes accessed | tf_op | source)
XLA Modules:
  0.0 78.4 jit_solution(14895062602107433375)
XLA Ops:
  0.0 0.0 copy-start
  0.0 76.7 %shard_map.73 = f32[256,256]{1,0:T(8,128)} custom-call(bf16[256,256]{1,0:T(8,128)(2,1)} %hid_hbm.1, bf16[4096]{0:T(1024)(128)(2,1)} %gain_in.1, bf16[4096,256]{1,0:T(8,128)(2,1)} %wq_hbm.1, bf16[128,256]{1,0:T(8,128)(2,1)} %keys_hbm.1, bf16[128,256]{1,0:T(8,128)(2,1)} %vals_hbm.1, s32[16]{0:T(128)} %len_ref.1, bf16[4096,256]{1,0:T(8,128)(2,1)} %wo_hbm.1), custom_call_target="tpu_custom_call" | custom-call | flops 6000000000 | bytes 8000000 | tf_op jit(solution)/shard_map/pallas_call | solution.py:447
  76.7 0.0 copy-done
  76.7 1.7 %convert_add_fusion = f32[256,256]{1,0:T(8,128)} fusion(f32[256,256]{1,0:T(8,128)} %shard_map.73, bf16[256,256]{1,0:T(8,128)(2,1)S(1)} %copy-done), kind=kLoop, calls=%fused_computation | loop fusion | flops 131072 | bytes 655360 | tf_op jit(solution)/shard_map/add | solution.py:484
Async XLA Ops:
  0.0 76.7 %copy-start = (bf16[256,256]{1,0:T(8,128)(2,1)S(1)}, bf16[256,256]{1,0:T(8,128)(2,1)}, u32[]{:S(2)}) copy-start(bf16[256,256]{1,0:T(8,128)(2,1)} %hid_hbm.1) | copy-start | bytes 393220

commit v6 on v5

--- a/solution.py
+++ b/solution.py
@@ -67,8 +67,6 @@
     for f in friends:
         pl.semaphore_signal(barrier, inc=1, device_id=f, device_id_type=MESH)
 
-    for o in range(SRC):
-        gain_ref[o] = gain_in[o * FEAT:(o + 1) * FEAT].astype(F32).reshape(1, FEAT)
     qacc[...] = jnp.zeros_like(qacc)
     ssq[...] = jnp.zeros_like(ssq)
     for c in loads[:3]:
@@ -176,6 +174,8 @@
         kv_push(tgt, u, (src, sib))
     inner = (yl > 0) & (yl < NYL - 1)
 
+    for o in range(SRC):
+        gain_ref[o] = gain_in[o * FEAT:(o + 1) * FEAT].astype(F32).reshape(1, FEAT)
     loads[3].wait()
     q_part(src)
 

time: 78.6 us -> 78.6 us (level)
  no operation moved by 1% of the time
where the time goes in v6:
time: 78.6 us; the launch traced here: 78.4 us
  Pallas kernels  76.7 us (98%)
  other arithmetic  1.68 us (2%)
    pallas_call x1, Pallas kernels, body(): pl.pallas_call(kernel, out_shape=jax.ShapeDtypeStruct((TOK, FEAT), F32),...  76.7 us
    add x1, other arithmetic, body(): return hidden_in.astype(F32) + branch  1.68 us

profile of v6, /device:TPU:2, one launch (start us, length us, event | category | flops | bytes accessed | tf_op | source)
XLA Modules:
  0.0 78.4 jit_solution(14829890554999349220)
XLA Ops:
  0.0 0.0 copy-start
  0.0 76.7 %shard_map.73 = f32[256,256]{1,0:T(8,128)} custom-call(bf16[256,256]{1,0:T(8,128)(2,1)} %hid_hbm.1, bf16[4096]{0:T(1024)(128)(2,1)} %gain_in.1, bf16[4096,256]{1,0:T(8,128)(2,1)} %wq_hbm.1, bf16[128,256]{1,0:T(8,128)(2,1)} %keys_hbm.1, bf16[128,256]{1,0:T(8,128)(2,1)} %vals_hbm.1, s32[16]{0:T(128)} %len_ref.1, bf16[4096,256]{1,0:T(8,128)(2,1)} %wo_hbm.1), custom_call_target="tpu_custom_call" | custom-call | flops 6000000000 | bytes 8000000 | tf_op jit(solution)/shard_map/pallas_call | solution.py:447
  76.7 0.0 copy-done
  76.7 1.7 %convert_add_fusion = f32[256,256]{1,0:T(8,128)} fusion(f32[256,256]{1,0:T(8,128)} %shard_map.73, bf16[256,256]{1,0:T(8,128)(2,1)S(1)} %copy-done), kind=kLoop, calls=%fused_computation | loop fusion | flops 131072 | bytes 655360 | tf_op jit(solution)/shard_map/add | solution.py:484
Async XLA Ops:
  0.0 76.7 %copy-start = (bf16[256,256]{1,0:T(8,128)(2,1)S(1)}, bf16[256,256]{1,0:T(8,128)(2,1)}, u32[]{:S(2)}) copy-start(bf16[256,256]{1,0:T(8,128)(2,1)} %hid_hbm.1) | copy-start | bytes 393220
